TPU v7x, 512 devices: a whole 4x4x16 slice. The times are simulated.
512 devices in a mesh: row: 32 (over y, x, core), col: 16 (over z).
Axes of the slice: x: 4, y: 4, z: 16, core: 2. Of those that a mesh axis runs over, the one named last changes fastest.
Arguments:
- points: bfloat16 [262144, 128], P(('row', 'col')), as said below
- noise: float32 [262144], P(('row', 'col')), may hold values from 1 to 4
- targets: float32 [262144, 16], P(('row', 'col')), as said below
- tile_rows: int32 [32, 16, 32], P('row', 'col'), may hold values from 0 to 511, as said below
- tile_cols: int32 [32, 16, 32], P('row', 'col'), may hold values from 0 to 511, as said below
- tile_count: int32 [32, 16], P('row', 'col'), may hold values from 0 to 32, as said below
Outputs:
- solution: float32 [262144, 16], P(('row', 'col'))
- residual: float32 [262144, 16], P(('row', 'col'))
Inputs may be any that keep to these rules, and one draw needn't show every extreme that they name: `tile_rows`: slot s of device (r, c) names row block r * 16 + a for some a below 16, and column block c plus a multiple of 16, never below the row block; no tile is named twice. `tile_cols`: column blocks of the slots, as described for tile_rows. Only the first tile_count slots of a device are tiles, the others are to be ignored; every device of row index 0 uses all 32 slots. `points`: Real-valued embeddings. `targets`: Real-valued right-hand sides.
All inputs are finite; a program needn't handle non-finite values.
Results may differ from a plain program's by a relative error of at most 0.0003.
Values may be sent and summed in bfloat16 or wider, within the bound.
A program may use at most 64 MiB of HBM per device.

v0:
```python
import math

import jax
import jax.numpy as jnp
from jax import lax
from jax.sharding import PartitionSpec as P

ITERS = 2


def wendland(left_pts, right_pts, left_norm, right_norm, radius):
    gram = lax.dot_general(
        left_pts, right_pts, (((1,), (1,)), ((), ())), preferred_element_type=jnp.float32
    )
    squared = jnp.maximum(left_norm[:, None] + right_norm[None, :] - 2.0 * gram, 0.0) + 1.0
    dist = jnp.sqrt(squared) / radius
    weight = jnp.maximum(1.0 - dist, 0.0)
    return weight**4 * (4.0 * dist + 1.0)


def norms(residual):
    return lax.psum(jnp.sum(residual * residual, axis=0), ("row", "col"))


def local(points, noise, targets, tile_rows, tile_cols, tile_count):
    width = points.shape[0]
    ncols = lax.axis_size("col")
    radius = 2.8 * math.sqrt(points.shape[1])
    signal = 2.0 / width
    row_pts = lax.all_gather(points, "col", axis=0, tiled=True)
    col_pts = lax.all_gather(points, "row", axis=0, tiled=True)
    row_square = jnp.sum(jnp.square(row_pts.astype(jnp.float32)), axis=1)
    col_square = jnp.sum(jnp.square(col_pts.astype(jnp.float32)), axis=1)
    rows = tile_rows[0, 0]
    cols = tile_cols[0, 0]
    count = tile_count[0, 0]
    rhs = targets.shape[1]
    solution = jnp.zeros_like(targets)
    residual = targets
    direction = targets
    norm_now = norms(residual)
    for step_index in range(ITERS):
        dir_row = lax.all_gather(direction, "col", axis=0, tiled=True)
        dir_col = lax.all_gather(direction, "row", axis=0, tiled=True)

        def one_tile(carry, slot):
            acc_row, acc_col, curv = carry
            i = rows[slot]
            j = cols[slot]
            start_a = i % ncols * width
            start_q = j // ncols * width
            used = jnp.where(slot < count, 1.0, 0.0).astype(jnp.float32)
            mirror = jnp.where(i != j, 1.0, 0.0).astype(jnp.float32)
            left_pts = lax.dynamic_slice_in_dim(row_pts, start_a, width, 0)
            right_pts = lax.dynamic_slice_in_dim(col_pts, start_q, width, 0)
            left_norm = lax.dynamic_slice_in_dim(row_square, start_a, width, 0)
            right_norm = lax.dynamic_slice_in_dim(col_square, start_q, width, 0)
            kernel = wendland(left_pts, right_pts, left_norm, right_norm, radius) * used
            left_vec = lax.dynamic_slice_in_dim(dir_row, start_a, width, 0)
            right_vec = lax.dynamic_slice_in_dim(dir_col, start_q, width, 0)
            forward = jnp.dot(
                kernel,
                right_vec,
                precision=lax.Precision.HIGHEST,
                preferred_element_type=jnp.float32,
            )
            backward = (
                lax.dot_general(
                    kernel,
                    left_vec,
                    (((0,), (0,)), ((), ())),
                    precision=lax.Precision.HIGHEST,
                    preferred_element_type=jnp.float32,
                )
                * mirror
            )
            old_row = lax.dynamic_slice_in_dim(acc_row, start_a, width, 0)
            acc_row = lax.dynamic_update_slice_in_dim(acc_row, old_row + forward, start_a, 0)
            old_col = lax.dynamic_slice_in_dim(acc_col, start_q, width, 0)
            acc_col = lax.dynamic_update_slice_in_dim(acc_col, old_col + backward, start_q, 0)
            return (acc_row, acc_col, curv)

        def group_step(group, carry):
            for offset in range(4):
                carry = one_tile(carry, group * 4 + offset)
            return carry

        start = (
            jnp.zeros((dir_row.shape[0], rhs), jnp.float32),
            jnp.zeros((dir_col.shape[0], rhs), jnp.float32),
            jnp.zeros((rhs,), jnp.float32),
        )
        acc_row, acc_col, curv = lax.fori_loop(0, (count + 3) // 4, group_step, start)
        row_total = lax.psum_scatter(acc_row, "col", scatter_dimension=0, tiled=True)
        col_total = lax.psum_scatter(acc_col, "row", scatter_dimension=0, tiled=True)
        image = noise[:, None] * direction + signal * (row_total + col_total)
        image, unused = (image, curv)
        curvature = lax.psum(jnp.sum(direction * image, axis=0), ("row", "col"))
        alpha = norm_now / curvature
        solution = solution + alpha * direction
        residual = residual - alpha * image
        fresh = norms(residual)
        direction = residual + fresh / norm_now * direction
        norm_now = fresh
    return (solution, residual)


def solution(mesh):
    return jax.shard_map(
        local,
        mesh=mesh,
        in_specs=(
            P(("row", "col"), None),
            P(("row", "col")),
            P(("row", "col"), None),
            P("row", "col", None),
            P("row", "col", None),
            P("row", "col"),
        ),
        out_specs=(P(("row", "col"), None), P(("row", "col"), None)),
        check_vma=False,
    )
```

profile of v0, /device:TPU:1, one launch (start us, length us, event | category | flops | bytes accessed | tf_op | source)
XLA Modules:
  0.0 1631.4 jit_solution(15980238654665216213)
XLA Ops:
  10.1 34.6 %all_gather.21 = f32[8192,16]{0,1:T(8,128)S(1)} all-gather(f32[512,16]{0,1:T(8,128)} %param.12), channel_id=1, replica_groups=mesh['row'=32,'col'=16] {'col'}, dimensions={0}, use_global_device_ids=true | all-gather | bytes 557056 | tf_op jit(solution)/shard_map/all_gather | solution.py:43
  44.7 35.7 %all-gather.5.cloned.1.call-done = bf16[8192,128]{1,0:T(8,128)(2,1)} async-done(((bf16[512,128]{1,0:T(8,128)(2,1)}), bf16[8192,128]{1,0:T(8,128)(2,1)}) %all-gather.5.cloned.1.call-update) | async-done | bytes 2097168 | tf_op jit(solution)/shard_map/all_gather | solution.py:30
  80.4 2.7 multiply_reduce_fusion.1
  83.2 67.8 %all-gather.7.cloned.1.call-done = bf16[16384,128]{1,0:T(8,128)(2,1)} async-done(((bf16[512,128]{1,0:T(8,128)(2,1)}), bf16[16384,128]{1,0:T(8,128)(2,1)}) %all-gather.7.cloned.1.call-update) | async-done | bytes 4194320 | tf_op jit(solution)/shard_map/all_gather | solution.py:31
  151.0 3.9 multiply_reduce_fusion
  154.9 56.9 %all-gather.9.cloned.1.call-done = f32[16384,16]{0,1:T(8,128)} async-done(((f32[512,16]{0,1:T(8,128)}), f32[16384,16]{0,1:T(8,128)}) %all-gather.9.cloned.1.call-update) | async-done | bytes 1048592 | tf_op jit(solution)/shard_map/all_gather | solution.py:44
  212.0 352.5 %while.30 = (s32[]{:T(128)}, f32[8192,16]{0,1:T(8,128)S(1)}, f32[16384,16]{0,1:T(8,128)S(1)}, s32[]{:T(128)}, s32[32]{0:T(128)S(1)}, /*index=5*/f32[8192]{0:T(10...) while((s32[]{:T(128)}, f32[8192,16]{0,1:T(8,128)S(1)}, ...), condition=%wide.region_5.6_spmd, body=%wide.region_4.5_spmd.sunk | while | flops 685867136 | bytes 14469353 | solution.py:93
  247.7 1.9 multiply_multiply_fusion.18
  291.7 1.9 multiply_multiply_fusion.18
  296.0 1.9 multiply_multiply_fusion.19
  335.8 1.9 multiply_multiply_fusion.18
  379.8 1.9 multiply_multiply_fusion.18
  384.1 1.9 multiply_multiply_fusion.19
  423.8 1.9 multiply_multiply_fusion.18
  467.9 1.9 multiply_multiply_fusion.18
  472.2 1.9 multiply_multiply_fusion.19
  511.9 1.9 multiply_multiply_fusion.18
  556.0 1.9 multiply_multiply_fusion.18
  566.0 55.7 %reduce-scatter.5.cloned.1.call-done = f32[512,16]{0,1:T(8,128)} async-done(((f32[8192,16]{0,1:T(8,128)}), f32[512,16]{0,1:T(8,128)}) %reduce-scatter.5.cloned.1.call-update) | async-done | bytes 32784 | tf_op jit(solution)/shard_map/reduce_scatter | solution.py:94
  621.7 112.5 %reduce-scatter.7.cloned.1.call-done = f32[512,16]{0,1:T(8,128)} async-done(((f32[16384,16]{0,1:T(8,128)}), f32[512,16]{0,1:T(8,128)}) %reduce-scatter.7.cloned.1.call-update) | async-done | bytes 32784 | tf_op jit(solution)/shard_map/reduce_scatter | solution.py:95
  735.1 105.4 %all-reduce = (f32[16]{0:T(128)S(1)}, f32[16]{0:T(128)S(1)}) all-reduce(f32[16]{0:T(128)S(1)} %get-tuple-element.459, f32[16]{0:T(128)S(1)} %get-tuple-element.458), channel_id=1, replica_groups=mesh['row'=32,'col'=16] {'row','col'}, use_global_device_ids=true, to_apply=%region_1.0 | all-reduce | flops 32 | bytes 256 | tf_op jit(solution)/shard_map/psum | solution.py:22
  841.5 99.4 %psum.30 = f32[16]{0:T(128)S(1)} all-reduce(f32[16]{0:T(128)S(1)} %get-tuple-element.514), channel_id=1, replica_groups=mesh['row'=32,'col'=16] {'row','col'}, use_global_device_ids=true, to_apply=%region_11.12 | all-reduce | flops 16 | bytes 128 | tf_op jit(solution)/shard_map/psum | solution.py:22
  941.7 23.5 %all_gather.23 = f32[8192,16]{0,1:T(8,128)S(1)} all-gather(f32[512,16]{0,1:T(8,128)} %multiply_add_fusion.2), channel_id=1, replica_groups=mesh['row'=32,'col'=16] {'col'}, dimensions={0}, use_global_device_ids=true | all-gather | bytes 557056 | tf_op jit(solution)/shard_map/all_gather | solution.py:43
  965.1 29.1 %all-gather.11.cloned.1.call-done = f32[16384,16]{0,1:T(8,128)} async-done(((f32[512,16]{0,1:T(8,128)}), f32[16384,16]{0,1:T(8,128)}) %all-gather.11.cloned.1.call-update) | async-done | bytes 1048592 | tf_op jit(solution)/shard_map/all_gather | solution.py:44
  994.3 352.5 %while.31 = (s32[]{:T(128)}, f32[8192,16]{0,1:T(8,128)S(1)}, f32[16384,16]{0,1:T(8,128)S(1)}, s32[]{:T(128)}, s32[32]{0:T(128)S(1)}, /*index=5*/f32[8192]{0:T(10...) while((s32[]{:T(128)}, f32[8192,16]{0,1:T(8,128)S(1)}, ...), condition=%wide.region_13.14_spmd, body=%wide.region_12.13_spmd.sunk | while | flops 685867136 | bytes 14469353 | solution.py:93
  1030.1 1.9 multiply_multiply_fusion.22
  1118.1 1.9 multiply_multiply_fusion.22
  1206.2 1.9 multiply_multiply_fusion.22
  1294.3 1.9 multiply_multiply_fusion.22
  1348.5 55.4 %reduce-scatter.9.cloned.1.call-done = f32[512,16]{0,1:T(8,128)} async-done(((f32[8192,16]{0,1:T(8,128)}), f32[512,16]{0,1:T(8,128)}) %reduce-scatter.9.cloned.1.call-update) | async-done | bytes 32784 | tf_op jit(solution)/shard_map/reduce_scatter | solution.py:94
  1403.9 112.9 %reduce-scatter.11.cloned.1.call-done = f32[512,16]{0,1:T(8,128)} async-done(((f32[16384,16]{0,1:T(8,128)}), f32[512,16]{0,1:T(8,128)}) %reduce-scatter.11.cloned.1.call-update) | async-done | bytes 32784 | tf_op jit(solution)/shard_map/reduce_scatter | solution.py:95
  1517.7 105.3 %psum.31 = f32[16]{0:T(128)S(1)} all-reduce(f32[16]{0:T(128)S(1)} %multiply_reduce_fusion.2), channel_id=1, replica_groups=mesh['row'=32,'col'=16] {'row','col'}, use_global_device_ids=true, to_apply=%region_17.18 | all-reduce | flops 16 | bytes 128 | tf_op jit(solution)/shard_map/psum | solution.py:98
  (271 shorter events, 279.2 us)
Async XLA Ops:
  7.2 73.3 %all-gather.5.cloned.1.call-start = ((), (), s32[]{:S(2)}) async-start(), calls=%async_computation.4 | async-start | bytes 2228224 | tf_op jit(solution)/shard_map/all_gather | solution.py:30
  7.9 143.1 %all-gather.7.cloned.1.call-start = ((), (), s32[]{:S(2)}) async-start(), calls=%async_computation.5 | async-start | bytes 4325376 | tf_op jit(solution)/shard_map/all_gather | solution.py:31
  8.6 203.2 %all-gather.9.cloned.1.call-start = ((), (), s32[]{:S(2)}) async-start(), calls=%async_computation.6 | async-start | bytes 1081344 | tf_op jit(solution)/shard_map/all_gather | solution.py:44
  9.4 612.3 %reduce-scatter.5.cloned.1.call-start = ((), (), s32[]{:S(2)}) async-start(), calls=%async_computation.7 | async-start | bytes 557056 | tf_op jit(solution)/shard_map/reduce_scatter | solution.py:94
  10.1 201.9 %copy-start.6 = (s32[1,1,32]{2,1,0:T(1,128)S(1)}, s32[1,1,32]{2,1,0:T(1,128)}, u32[]{:S(2)}) copy-start(s32[1,1,32]{2,1,0:T(1,128)} %param.13) | copy-start | bytes 388
  10.1 201.9 %copy-start.7 = (s32[1,1,32]{2,1,0:T(1,128)S(1)}, s32[1,1,32]{2,1,0:T(1,128)}, u32[]{:S(2)}) copy-start(s32[1,1,32]{2,1,0:T(1,128)} %param.14) | copy-start | bytes 388
  212.0 522.3 %copy-start.4 = (f32[512,16]{0,1:T(8,128)S(1)}, f32[512,16]{0,1:T(8,128)}, u32[]{:S(2)}) copy-start(f32[512,16]{0,1:T(8,128)} %param.12) | copy-start | bytes 98308
  212.0 522.2 %copy-start.8 = (f32[512]{0:T(512)S(1)}, f32[512]{0:T(512)}, u32[]{:S(2)}) copy-start(f32[512]{0:T(512)} %param.11) | copy-start | bytes 6148
  564.5 0.8 copy-start.2
  564.5 1.2 copy-start
  565.3 168.9 %reduce-scatter.7.cloned.1.call-start = ((), (), s32[]{:S(2)}) async-start(), calls=%async_computation.8 | async-start | bytes 1081344 | tf_op jit(solution)/shard_map/reduce_scatter | solution.py:95
  565.9 428.3 %all-gather.11.cloned.1.call-start = ((), (), s32[]{:S(2)}) async-start(), calls=%async_computation.9 | async-start | bytes 1081344 | tf_op jit(solution)/shard_map/all_gather | solution.py:44
  941.6 462.3 %reduce-scatter.9.cloned.1.call-start = ((), (), s32[]{:S(2)}) async-start(), calls=%async_computation.10 | async-start | bytes 557056 | tf_op jit(solution)/shard_map/reduce_scatter | solution.py:94
  994.3 522.5 %copy-start.5 = (f32[512,16]{0,1:T(8,128)S(1)}, f32[512,16]{0,1:T(8,128)}, u32[]{:S(2)}) copy-start(f32[512,16]{0,1:T(8,128)} %multiply_add_fusion.2) | copy-start | bytes 98308
  1346.9 0.8 copy-start.3
  1346.9 1.2 copy-start.1
  1347.7 169.1 %reduce-scatter.11.cloned.1.call-start = ((), (), s32[]{:S(2)}) async-start(), calls=%async_computation.11 | async-start | bytes 1081344 | tf_op jit(solution)/shard_map/reduce_scatter | solution.py:95
Sparse Core Ops, SparseCore 0:
  10.1 70.3 all-gather.4
  83.6 67.3 all-gather.6
  154.2 57.6 all-gather.8
  565.5 56.2 reduce-scatter.4
  626.6 107.6 reduce-scatter.6
  941.7 52.4 all-gather.10
  1347.8 55.9 reduce-scatter.8
  1408.9 107.8 reduce-scatter.10
where the time goes:
time: 1640 us; the launch traced here: 1630 us
  waiting for transfers between devices  529 us (32%)
  loops' own time  408 us (25%)
  blocking collectives  368 us (22%)
  matrix products  273 us (17%)
  local copies, waits for them, and re-layouts  25.9 us (2%)
    another operation x2, loops' own time, local(): lax.fori_loop(0, (count + 3) // 4, group_step, start)  408 us
    reduce_scatter x2, waiting for transfers between devices, local(): lax.psum_scatter(acc_col, 'row', scatter_dimension=0, tiled=True)  225 us
    psum x2, blocking collectives, norms(): return lax.psum(jnp.sum(residual * residual, axis=0), ('row', 'col'))  205 us
    dot_general x64, matrix products, wendland(): lax.dot_general(left_pts, right_pts, (((1,), (1,)), ((), ())), preferred_...  119 us
    dot_general x64, matrix products, one_tile(): jnp.dot(kernel, right_vec, precision=lax.Precision.HIGHEST, preferred_ele...  112 us
    reduce_scatter x2, waiting for transfers between devices, local(): lax.psum_scatter(acc_row, 'col', scatter_dimension=0, tiled=True)  111 us
    psum x1, blocking collectives, local(): curvature = lax.psum(jnp.sum(direction * image, axis=0), ('row', 'col'))  105 us
    all_gather x2, waiting for transfers between devices, local(): dir_col = lax.all_gather(direction, 'row', axis=0, tiled=True)  86 us
  transfers between devices with their start and end apart: 8, of which 8 were waited for; matrix products, arithmetic and copies ran while one was open for 0% of the time, Pallas kernels for 0%

commit v1 on v0

v1 whole, which is shorter than its diff:
```python
import functools
import math

import jax
import jax.numpy as jnp
from jax import lax
from jax.experimental import pallas as pl
from jax.experimental.pallas import tpu as pltpu
from jax.sharding import PartitionSpec as P

MESH = pl.DeviceIdType.MESH
F32, BF16 = jnp.float32, jnp.bfloat16
NT = (((1,), (1,)), ((), ()))
NN = (((1,), (0,)), ((), ()))
NR, NC = 32, 16
SIDE = 4
SLOTS = 32
RHS = 16


def kernel(radius, scale, pts, noise, t, rows, cols, count, sol, res,
           rp, ra, cp, ca, khi, klo, vr0, vc0, vr1, vc1, wr, wc, fs, bs,
           rpart0, cpart0, rpart1, cpart1, za0, zb0, zm0, xi0, za1, zb1, zm1, xi1,
           arz0, arx0, arz1, arx1, arz2, arx2,
           ring_s, ring_r, xy_s, xy_r, gz_s, gz_r, gx_s, gx_r, sz_s, sz_r, sx_s, sx_r, ar_s, ar_r):
    r = lax.axis_index("row")
    c = lax.axis_index("col")
    core = lax.rem(r, 2)
    yx = r // 2
    y = yx // SIDE
    x = lax.rem(yx, SIDE)

    def zdev(k):
        return (r, lax.rem(c + (k + NC), NC))

    def zidx(k):
        return lax.rem(c + (k + NC), NC)

    def rdma(src, dst, ssem, rsem, where):
        return pltpu.make_async_remote_copy(
            src_ref=src, dst_ref=dst, send_sem=ssem, recv_sem=rsem, device_id=where, device_id_type=MESH)

    def drain(ref, sem):
        pltpu.make_async_copy(ref, ref, sem).wait()

    barrier = pltpu.get_barrier_semaphore()

    def greet_z(k, carry):
        pl.semaphore_signal(barrier, inc=1, device_id=(r, lax.rem(c + k, NC)), device_id_type=MESH)
        return carry

    def greet_x(k, carry):
        pl.semaphore_signal(barrier, inc=1, device_id=(lax.rem(r + k, NR), c), device_id_type=MESH)
        return carry

    lax.fori_loop(1, NC, greet_z, 0)
    lax.fori_loop(1, NR, greet_x, 0)

    points = pts[...]
    half = points.shape[0] // 2
    rp[c] = points
    scaled = -2.0 * points
    cp[0, core, y, x] = scaled[:half]
    cp[1, core, y, x] = scaled[half:]
    vr0[c] = t[...]
    vc0[r] = t[...]
    pl.semaphore_wait(barrier, NC - 1 + NR - 1)

    def ring_send(d, s):
        sign = 1 - 2 * d
        block = zidx(-sign * s)
        for ch in range(2):
            if s == 7 and ch != d:
                continue
            part = rp.at[block, pl.ds(ch * half, half)]
            rdma(part, part, ring_s.at[d, s, ch], ring_r.at[d, s, ch], zdev(sign)).start()

    def ring_wait(d, s):
        sign = 1 - 2 * d
        block = zidx(-sign * (s + 1))
        for ch in range(2):
            if s == 7 and ch != d:
                continue
            part = rp.at[block, pl.ds(ch * half, half)]
            rdma(part, part, ring_s.at[d, s, ch], ring_r.at[d, s, ch], zdev(sign)).wait_recv()

    def ring_forward(d, s):
        sign = 1 - 2 * d
        block = zidx(-sign * s)
        for ch in range(2):
            part = rp.at[block, pl.ds(ch * half, half)]
            rdma(part, part, ring_s.at[d, s - 1, ch], ring_r.at[d, s - 1, ch], zdev(sign)).wait_recv()
            if s == 7 and ch != d:
                continue
            rdma(part, part, ring_s.at[d, s, ch], ring_r.at[d, s, ch], zdev(sign)).start()

    def xdev(k):
        return ((y * SIDE + lax.rem(x + k, SIDE)) * 2 + core, c)

    def ydev(k):
        return ((lax.rem(y + k, SIDE) * SIDE + x) * 2 + core, c)

    other = (r + 1 - 2 * core, c)

    def wide(h, k, p, ref):
        return ref.at[0, k, p] if h == 0 else ref.at[1, k, :, p]

    def xy_first(h, k):
        mine = cp.at[h, core, y, x]
        return rdma(mine, mine, xy_s.at[h, 0, k], xy_r.at[h, 0, k], xdev(k) if h == 0 else ydev(k))

    def xy_second(h, k):
        group = wide(h, core, y if h == 0 else x, cp)
        return rdma(group, group, xy_s.at[h, 1, k], xy_r.at[h, 1, k], ydev(k) if h == 0 else xdev(k))

    def xy_third(h, k):
        place = lax.rem((y if h == 0 else x) + (SIDE - k), SIDE)
        group = wide(h, core, place, cp)
        return rdma(group, group, xy_s.at[h, 2, k], xy_r.at[h, 2, k], other)

    lane = lax.broadcasted_iota(jnp.int32, (half, 128), 1)

    def features(block, first, weight):
        wide32 = block.astype(F32)
        norm = jnp.sum(wide32 * wide32, axis=1, keepdims=True) * weight
        if not first:
            norm = norm + 1.0
        hi = norm.astype(BF16).astype(F32)
        mid = (norm - hi).astype(BF16).astype(F32)
        low = norm - hi - mid
        at = 0 if first else 3
        out = jnp.where(lane == at, hi, jnp.where(lane == at + 1, mid, jnp.where(lane == at + 2, low, 0.0)))
        one = 3 if first else 0
        out = jnp.where((lane >= one) & (lane < one + 3), 1.0, out)
        return out.astype(BF16)

    def row_features(block):
        for ch in range(2):
            part = pl.ds(ch * half, half)
            ra[block, part] = features(rp[block, part], True, 1.0)

    def col_features(h, k, p):
        for m in range(SIDE):
            if h == 0:
                ca[0, k, p, m] = features(cp[0, k, p, m], False, 0.25)
            else:
                ca[1, k, m, p] = features(cp[1, k, m, p], False, 0.25)

    for d in range(2):
        ring_send(d, 0)
    for k in (1, 3, 2):
        for h in range(2):
            xy_first(h, k).start()
    row_features(c)
    for d in range(2):
        ring_forward(d, 1)
    for h in range(2):
        for k in (1, 3, 2):
            xy_first(h, k).wait_recv()
        for k in (1, 3, 2):
            xy_second(h, k).start()
        xy_third(h, 0).start()
    for d in range(2):
        ring_forward(d, 2)
    for h in range(2):
        col_features(h, core, y if h == 0 else x)
    for d in range(2):
        ring_forward(d, 3)
    for d in range(2):
        for s in (1, 2):
            row_features(zidx(-(1 - 2 * d) * s))
    for h in range(2):
        xy_third(h, 0).wait_recv()
        col_features(h, 1 - core, y if h == 0 else x)
    for d in range(2):
        ring_forward(d, 4)
    for h in range(2):
        for k in (1, 3):
            xy_second(h, k).wait_recv()
            xy_third(h, k).start()
            col_features(h, core, lax.rem((y if h == 0 else x) + (SIDE - k), SIDE))
    for d in range(2):
        ring_forward(d, 5)
    for d in range(2):
        for s in (3, 4):
            row_features(zidx(-(1 - 2 * d) * s))
    for h in range(2):
        xy_second(h, 2).wait_recv()
        xy_third(h, 2).start()
    for d in range(2):
        ring_forward(d, 6)
    for h in range(2):
        col_features(h, core, lax.rem((y if h == 0 else x) + 2, SIDE))
    for h in range(2):
        for k in (1, 3):
            xy_third(h, k).wait_recv()
            col_features(h, 1 - core, lax.rem((y if h == 0 else x) + (SIDE - k), SIDE))
    for d in range(2):
        ring_forward(d, 7)

    def gather_z(n, buf):
        for d in range(2):
            for k in (4, 3, 2, 1):
                rdma(buf.at[c], buf.at[c], gz_s.at[n, d, k - 1], gz_r.at[n, d, k - 1], zdev((1 - 2 * d) * k)).start()

    def gather_z_far(n, d, k, buf):
        block = zidx(-(1 - 2 * d) * 4)
        part = buf.at[block] if k < 4 else buf.at[block, pl.ds(8 * d, 8)]
        return rdma(part, part, gz_s.at[n, d, 3 + k], gz_r.at[n, d, 3 + k], zdev((1 - 2 * d) * k))

    def gather_z_forward(n, buf):
        for d in range(2):
            rdma(buf.at[c], buf.at[c], gz_s.at[n, d, 3], gz_r.at[n, d, 3], zdev((1 - 2 * d) * 4)).wait_recv()
            for k in (4, 3, 2, 1):
                gather_z_far(n, d, k, buf).start()

    def gather_z_finish(n, buf):
        for d in range(2):
            for k in (1, 2, 3):
                rdma(buf.at[c], buf.at[c], gz_s.at[n, d, k - 1], gz_r.at[n, d, k - 1], zdev((1 - 2 * d) * k)).wait_recv()
            for k in (1, 2, 3, 4):
                gather_z_far(n, d, k, buf).wait_recv()

    def gather_z_sent(n, buf):
        for d in range(2):
            for k in (1, 2, 3, 4):
                rdma(buf.at[c], buf.at[c], gz_s.at[n, d, k - 1], gz_r.at[n, d, k - 1], zdev((1 - 2 * d) * k)).wait_send()
                gather_z_far(n, d, k, buf).wait_send()

    def gather_x(n, buf):
        def send(k, carry):
            rdma(buf.at[r], buf.at[r], gx_s.at[n], gx_r.at[n], (lax.rem(r + k, NR), c)).start()
            return carry
        lax.fori_loop(1, NR, send, 0)

    def place(d, k):
        return zidx((1 - 2 * d) * k)

    def scatter_z_far(n, d, k, part, za):
        block = place(d, k + 4)
        src = part.at[block] if k < 4 else part.at[block, pl.ds(8 * d, 8)]
        dst = za.at[d, k - 1] if k < 4 else za.at[d, 3, pl.ds(8 * d, 8)]
        return rdma(src, dst, sz_s.at[n, d, 3 + k], sz_r.at[n, d, 3 + k], zdev((1 - 2 * d) * k))

    def scatter_z_near(n, d, k, part, zb, zm):
        src = part.at[place(d, k)] if k < 4 else zm.at[d]
        return rdma(src, zb.at[d, k - 1], sz_s.at[n, d, k - 1], sz_r.at[n, d, k - 1], zdev((1 - 2 * d) * k))

    def scatter_z(n, part, za, zb, zm):
        for k in (4, 3, 2, 1):
            for d in range(2):
                scatter_z_far(n, d, k, part, za).start()
        for k in (3, 2, 1):
            for d in range(2):
                scatter_z_near(n, d, k, part, zb, zm).start()

    def scatter_z_forward(n, part, za, zb, zm):
        for d in range(2):
            for k in (1, 2, 3, 4):
                scatter_z_far(n, d, k, part, za).wait_recv()
            zm[d] = part[place(d, 4)] + za[d, 0] + za[d, 1] + za[d, 2]
            rowpart = pl.ds(8 * d, 8)
            zm[d, rowpart] = zm[d, rowpart] + za[d, 3, rowpart]
            scatter_z_near(n, d, 4, part, zb, zm).start()

    def scatter_z_finish(n, part, zb, zm):
        total = part[c]
        for k in (1, 2, 3, 4):
            for d in range(2):
                scatter_z_near(n, d, k, part, zb, zm).wait_recv()
                total = total + zb[d, k - 1]
        return total

    def scatter_z_sent(n, part, za, zb, zm):
        for d in range(2):
            for k in (1, 2, 3, 4):
                scatter_z_far(n, d, k, part, za).wait_send()
                scatter_z_near(n, d, k, part, zb, zm).wait_send()

    def scatter_x(n, part, xi):
        def send(k, carry):
            to = lax.rem(r + k, NR)
            rdma(part.at[to], xi.at[r], sx_s.at[n], sx_r.at[n], (to, c)).start()
            return carry
        lax.fori_loop(1, NR, send, 0)
        xi[r] = part[r]

    def scatter_x_finish(n, xi):
        drain(xi.at[pl.ds(0, NR - 1)], sx_r.at[n])
        return lax.fori_loop(1, NR, lambda k, total: total + xi[k], xi[0])

    def reduce_z(n, value, arz):
        arz[c] = jnp.broadcast_to(value, (RHS, 128))

        def send(k, carry):
            rdma(arz.at[c], arz.at[c], ar_s.at[n, 0], ar_r.at[n, 0], (r, lax.rem(c + k, NC))).start()
            return carry
        lax.fori_loop(1, NC, send, 0)

    def reduce_x(n, arz, arx):
        drain(arz.at[pl.ds(0, NC - 1)], ar_r.at[n, 0])
        arx[r] = lax.fori_loop(1, NC, lambda k, total: total + arz[k], arz[0])

        def send(k, carry):
            rdma(arx.at[r], arx.at[r], ar_s.at[n, 1], ar_r.at[n, 1], (lax.rem(r + k, NR), c)).start()
            return carry
        lax.fori_loop(1, NR, send, 0)

    def reduce_finish(n, arx):
        drain(arx.at[pl.ds(0, NR - 1)], ar_r.at[n, 1])
        return lax.fori_loop(1, NR, lambda k, total: total + arx[k], arx[0])

    def reduce_sent(n, arz, arx):
        drain(arz.at[pl.ds(0, NC - 1)], ar_s.at[n, 0])
        drain(arx.at[pl.ds(0, NR - 1)], ar_s.at[n, 1])

    def tile_at(s):
        return lax.rem(rows[0, 0, s], NC), cols[0, 0, s] // NC

    def make_tile(s, carry):
        a, q = tile_at(s)
        k, pos = lax.rem(q, 2), q // 2
        qy, qx = pos // SIDE, lax.rem(pos, SIDE)
        right = jnp.concatenate([
            jnp.concatenate([cp[h, k, qy, qx], ca[h, k, qy, qx]], axis=1) for h in range(2)], axis=0)
        for h in range(2):
            part = pl.ds(h * half, half)
            left = jnp.concatenate([rp[a, part], ra[a, part]], axis=1)
            squared = jnp.maximum(lax.dot_general(left, right, NT, preferred_element_type=F32), 1.0)
            dist = squared * lax.rsqrt(squared)
            w = jnp.maximum(radius - dist, 0.0)
            w = w * w
            value = w * w * (dist + 0.25 * radius)
            hi = value.astype(BF16)
            khi[s, part] = hi
            klo[s, part] = (value - hi.astype(F32)).astype(BF16)
        return carry

    def split(v):
        hi = v.astype(BF16)
        return jnp.concatenate([hi, (v - hi.astype(F32)).astype(BF16)], axis=0)

    def apply(v, s, dims):
        both = lax.dot_general(v, khi[s], dims, preferred_element_type=F32)
        low = lax.dot_general(v[:RHS], klo[s], dims, preferred_element_type=F32)
        return both[:RHS] + both[RHS:] + low

    def forward(s, carry):
        a, q = tile_at(s)
        fs[s] = apply(wc[q], s, NT)
        return carry

    def backward(s, carry):
        a, q = tile_at(s)
        bs[s] = apply(wr[a], s, NN)
        return carry

    used = count[0, 0]

    def sum_rows(part):
        def one(a, carry):
            def add(s, total):
                hit = (tile_at(s)[0] == a) & (s < used)
                return total + jnp.where(hit, fs[s], 0.0)
            part[a] = lax.fori_loop(0, SLOTS, add, jnp.zeros((RHS, 2 * half), F32), unroll=8)
            return carry
        lax.fori_loop(0, NC, one, 0)

    def sum_cols(part):
        def one(q, carry):
            def add(s, total):
                hit = (tile_at(s)[1] == q) & (s < used) & (rows[0, 0, s] != cols[0, 0, s])
                return total + jnp.where(hit, bs[s], 0.0)
            part[q] = lax.fori_loop(0, SLOTS, add, jnp.zeros((RHS, 2 * half), F32), unroll=8)
            return carry
        lax.fori_loop(0, NR, one, 0)

    def curvature(vec):
        def add(s, total):
            a, q = tile_at(s)
            weight = jnp.where(rows[0, 0, s] != cols[0, 0, s], 2.0, 1.0)
            return total + jnp.where(s < used, weight * (vec(a) * fs[s]), 0.0)
        return lax.fori_loop(0, SLOTS, add, jnp.zeros((RHS, 2 * half), F32))

    def along(value):
        return jnp.sum(value, axis=1, keepdims=True)

    column = lax.broadcasted_iota(jnp.int32, (RHS, 128), 1)

    def pick(tile, n):
        return along(jnp.where(column == n, tile, 0.0))

    gather_z(0, vr0)
    gather_x(0, vc0)
    for d in range(2):
        for s in (5, 6):
            row_features(zidx(-(1 - 2 * d) * s))
    for h in range(2):
        xy_third(h, 2).wait_recv()
        col_features(h, 1 - core, lax.rem((y if h == 0 else x) + 2, SIDE))
    row_features(zidx(7))
    row_features(zidx(-7))
    for d in range(2):
        ring_wait(d, 7)
    row_features(zidx(8))
    lax.fori_loop(0, SLOTS // 2, make_tile, 0)
    gather_z_forward(0, vr0)
    lax.fori_loop(SLOTS // 2, SLOTS, make_tile, 0)
    gather_z_finish(0, vr0)
    drain(vc0.at[pl.ds(0, NR - 1)], gx_r.at[0])

    def split_row(a, carry):
        wr[a] = split(vr0[a])
        return carry

    def split_col(q, carry):
        wc[q] = split(vc0[q])
        return carry

    lax.fori_loop(0, NR, split_col, 0)
    lax.fori_loop(0, SLOTS, forward, 0)
    sum_rows(rpart0)
    scatter_z(0, rpart0, za0, zb0, zm0)
    target = t[...]
    curve = scale * along(curvature(lambda a: vr0[a])) + along(noise[...] * target * target)
    reduce_z(0, jnp.where(column == 0, curve, along(target * target)), arz0)
    lax.fori_loop(0, NC, split_row, 0)
    lax.fori_loop(0, SLOTS, backward, 0)
    sum_cols(cpart0)
    scatter_x(0, cpart0, xi0)
    scatter_z_forward(0, rpart0, za0, zb0, zm0)
    reduce_x(0, arz0, arx0)
    image = scatter_z_finish(0, rpart0, zb0, zm0)
    image = noise[...] * target + scale * (image + scatter_x_finish(0, xi0))
    sums = reduce_finish(0, arx0)
    norm0 = pick(sums, 1)
    alpha0 = norm0 / pick(sums, 0)
    res[...] = target - alpha0 * image
    vr1[c] = res[...]
    vc1[r] = res[...]

    gather_z(1, vr1)
    gather_x(1, vc1)
    reduce_z(1, along(res[...] * res[...]), arz1)
    gather_z_forward(1, vr1)
    reduce_x(1, arz1, arx1)
    norm1 = pick(reduce_finish(1, arx1), 0)
    beta = norm1 / norm0
    drain(vc1.at[pl.ds(0, NR - 1)], gx_r.at[1])

    def direct_col(q, carry):
        wc[q] = split(vc1[q] + beta * vc0[q])
        return carry

    def direct_row(a, carry):
        v = vr1[a] + beta * vr0[a]
        vr1[a] = v
        wr[a] = split(v)
        return carry

    lax.fori_loop(0, NR, direct_col, 0)
    lax.fori_loop(0, SLOTS, forward, 0)
    sum_rows(rpart1)
    scatter_z(1, rpart1, za1, zb1, zm1)
    gather_z_finish(1, vr1)
    gather_z_sent(1, vr1)
    residual = res[...]
    lax.fori_loop(0, NC, direct_row, 0)
    direction = residual + beta * target
    curve = scale * along(curvature(lambda a: vr1[a])) + along(noise[...] * direction * direction)
    reduce_z(2, curve, arz2)
    lax.fori_loop(0, SLOTS, backward, 0)
    sum_cols(cpart1)
    scatter_x(1, cpart1, xi1)
    scatter_z_forward(1, rpart1, za1, zb1, zm1)
    reduce_x(2, arz2, arx2)
    image = scatter_z_finish(1, rpart1, zb1, zm1)
    image = noise[...] * direction + scale * (image + scatter_x_finish(1, xi1))
    alpha1 = norm1 / pick(reduce_finish(2, arx2), 0)
    sol[...] = alpha0 * target + alpha1 * direction
    res[...] = residual - alpha1 * image

    for d in range(2):
        for s in range(8):
            for ch in range(2):
                if s == 7 and ch != d:
                    continue
                part = rp.at[0, pl.ds(0, half)]
                rdma(part, part, ring_s.at[d, s, ch], ring_r.at[d, s, ch], zdev(1)).wait_send()
    for h in range(2):
        for k in (1, 2, 3):
            xy_first(h, k).wait_send()
            xy_second(h, k).wait_send()
        for k in range(4):
            xy_third(h, k).wait_send()
    gather_z_sent(0, vr0)
    drain(vc0.at[pl.ds(0, NR - 1)], gx_s.at[0])
    drain(vc1.at[pl.ds(0, NR - 1)], gx_s.at[1])
    scatter_z_sent(0, rpart0, za0, zb0, zm0)
    scatter_z_sent(1, rpart1, za1, zb1, zm1)
    drain(xi0.at[pl.ds(0, NR - 1)], sx_s.at[0])
    drain(xi1.at[pl.ds(0, NR - 1)], sx_s.at[1])
    reduce_sent(0, arz0, arx0)
    reduce_sent(1, arz1, arx1)
    reduce_sent(2, arz2, arx2)


def local(points, noise, targets, tile_rows, tile_cols, tile_count):
    block, width = points.shape
    radius = 2.8 * math.sqrt(width)
    scale = 2.0 / block * 4.0 / radius**5
    half = block // 2
    vmem = pl.BlockSpec(memory_space=pltpu.VMEM)
    smem = pl.BlockSpec(memory_space=pltpu.SMEM)
    vec = jax.ShapeDtypeStruct((RHS, block), F32)
    dma = pltpu.SemaphoreType.DMA

    def vecs(*lead):
        return pltpu.VMEM((*lead, RHS, block), F32)

    sol, res = pl.pallas_call(
        functools.partial(kernel, radius, scale),
        out_shape=(vec, vec),
        in_specs=[vmem, vmem, vmem, smem, smem, smem],
        out_specs=(vmem, vmem),
        scratch_shapes=[
            pltpu.VMEM((NC, block, width), BF16),
            pltpu.VMEM((NC, block, width), BF16),
            pltpu.VMEM((2, 2, SIDE, SIDE, half, width), BF16),
            pltpu.VMEM((2, 2, SIDE, SIDE, half, width), BF16),
            pltpu.VMEM((SLOTS, block, block), BF16),
            pltpu.VMEM((SLOTS, block, block), BF16),
            vecs(NC), vecs(NR), vecs(NC), vecs(NR),
            pltpu.VMEM((NC, 2 * RHS, block), BF16),
            pltpu.VMEM((NR, 2 * RHS, block), BF16),
            vecs(SLOTS), vecs(SLOTS),
            vecs(NC), vecs(NR), vecs(NC), vecs(NR),
            vecs(2, 4), vecs(2, 4), vecs(2), vecs(NR),
            vecs(2, 4), vecs(2, 4), vecs(2), vecs(NR),
            *[pltpu.VMEM((n, RHS, 128), F32) for n in (NC, NR) * 3],
            dma((2, 8, 2)), dma((2, 8, 2)),
            dma((2, 3, 4)), dma((2, 3, 4)),
            dma((2, 2, 8)), dma((2, 2, 8)),
            dma((2,)), dma((2,)),
            dma((2, 2, 8)), dma((2, 2, 8)),
            dma((2,)), dma((2,)),
            dma((3, 2)), dma((3, 2)),
        ],
        compiler_params=pltpu.CompilerParams(
            collective_id=0, has_side_effects=True, vmem_limit_bytes=60 * 1024 * 1024),
    )(points, noise[None, :], targets.T, tile_rows, tile_cols, tile_count)
    return sol.T, res.T


def solution(mesh):
    return jax.shard_map(
        local,
        mesh=mesh,
        in_specs=(
            P(("row", "col"), None),
            P(("row", "col")),
            P(("row", "col"), None),
            P("row", "col", None),
            P("row", "col", None),
            P("row", "col"),
        ),
        out_specs=(P(("row", "col"), None), P(("row", "col"), None)),
        check_vma=False,
    )
```

time: 1640 us -> 208 us (0.13)
  waiting for transfers between devices: 529 us -> 0 us
  loops' own time: 408 us -> 0 us
  blocking collectives: 368 us -> 0 us
  matrix products: 273 us -> 0 us
  Pallas kernels: 0 us -> 204 us
  local copies, waits for them, and re-layouts: 25.9 us -> 2 us
    another operation x2 -> x0, loops' own time: 408 us -> none  [local(): lax.fori_loop(0, (count + 3) // 4, group_step, start)]
    reduce_scatter x4 -> x0, waiting for transfers between devices: 337 us -> none  [the longest x2 225 us: local(): lax.psum_scatter(acc_col, 'row', scatter_dimension=0, tiled=True)]
    psum x3 -> x0, blocking collectives: 310 us -> none  [the longest x2 205 us: norms(): return lax.psum(jnp.sum(residual * residual, axis=0), ('row', 'col'))]
    dot_general x192 -> x0, matrix products: 273 us -> none  [the longest x64 119 us: wendland(): lax.dot_general(left_pts, right_pts, (((1,), (1,)), ((), ())), preferred_...]
    pallas_call x0 -> x1, Pallas kernels: none -> 204 us  [local(): pl.pallas_call(functools.partial(kernel, radius, scale), out_shape=(vec,...]
    all_gather x4 -> x0, waiting for transfers between devices: 190 us -> none  [the longest x2 86 us: local(): dir_col = lax.all_gather(direction, 'row', axis=0, tiled=True)]
    all_gather x2 -> x0, blocking collectives: 58.1 us -> none  [local(): dir_row = lax.all_gather(direction, 'col', axis=0, tiled=True)]
    dynamic_slice x48 -> x0, local copies, waits for them, and re-layouts: 23.4 us -> none  [the longest x16 11 us: one_tile(): i = rows[slot]]
  transfers between devices with their start and end apart: 8 -> 0, of which waited for: 8 -> 0; matrix products, arithmetic and copies ran while one was open for 0% -> 0% of each run, Pallas kernels for 0% -> 0%
where the time goes in v1:
time: 208 us
  Pallas kernels  204 us (98%)
    pallas_call x1, Pallas kernels, local(): pl.pallas_call(functools.partial(kernel, radius, scale), out_shape=(vec,...  204 us

profile of v1, /device:TPU:1, one launch (start us, length us, event | category | flops | bytes accessed | tf_op | source)
XLA Modules:
  0.0 207.6 jit_solution(11482461070986051739)
XLA Ops:
  1.3 204.3 %shard_map.77 = (f32[16,512]{1,0:T(8,128)}, f32[16,512]{1,0:T(8,128)}) custom-call(bf16[512,128]{1,0:T(8,128)(2,1)} %pts.1, f32[1,512]{1,0:T(1,128)} %bitcast.7, f32[16,512]{1,0:T(8,128)} %bitcast.6, s32[1,1,32]{2,1,0:T(1,128)} %rows.1, s32[1,1,32]{2,1,0:T(1,128)} %cols.1, s32[1,1]{1,0:T(1,128)S(6)} %copy.10.count), custom_call_target="tpu_custom_call" | custom-call | tf_op jit(solution)/shard_map/pallas_call | solution.py:521
  205.6 0.0 copy-start
  205.6 1.4 copy.11
  207.0 0.0 copy-done
  207.0 0.6 copy.12
Async XLA Ops:
  205.6 1.4 copy-start

commit v2 on v1

v2 whole, which is shorter than its diff:
```python
import functools
import math

import jax
import jax.numpy as jnp
from jax import lax
from jax.experimental import pallas as pl
from jax.experimental.pallas import tpu as pltpu
from jax.sharding import PartitionSpec as P

MESH = pl.DeviceIdType.MESH
F32, BF16 = jnp.float32, jnp.bfloat16
NT = (((1,), (1,)), ((), ()))
NN = (((1,), (0,)), ((), ()))
NR, NC = 32, 16
SIDE = 4
SLOTS = 32
RHS = 16
PIECES = 4


def kernel(radius, scale, pts, noise, t, meta, sol, res,
           rp, ra, cp, ca, khi, klo, vr0, vc0, vr1, vc1, wr, wc, fs, bs,
           rpart0, cpart0, rpart1, cpart1, za0, zb0, zm0, xs0, xi0, za1, zb1, zm1, xs1, xi1,
           arz0, ars0, arx0, arz1, ars1, arx1,
           ring_s, ring_r, xy_s, xy_r, gz_s, gz_r, gx_s, gx_r, sz_s, sz_r, sx_s, sx_r, ar_s, ar_r):
    r = lax.axis_index("row")
    c = lax.axis_index("col")
    core = lax.rem(r, 2)
    yx = r // 2
    y = yx // SIDE
    x = lax.rem(yx, SIDE)

    def zdev(k):
        return (r, lax.rem(c + (k + NC), NC))

    def zidx(k):
        return lax.rem(c + (k + NC), NC)

    def rdma(src, dst, ssem, rsem, where):
        return pltpu.make_async_remote_copy(
            src_ref=src, dst_ref=dst, send_sem=ssem, recv_sem=rsem, device_id=where, device_id_type=MESH)

    def total_of(parts):
        while len(parts) > 1:
            parts = [sum(parts[k:k + 2][1:], parts[k]) for k in range(0, len(parts), 2)]
        return parts[0]

    def drain(ref, sem):
        pltpu.make_async_copy(ref, ref, sem).wait()

    barrier = pltpu.get_barrier_semaphore()

    def greet(where):
        pl.semaphore_signal(barrier, inc=1, device_id=where, device_id_type=MESH)

    def row_dev(k):
        return (lax.rem(yx + k, NR // 2) * 2 + core, c)

    other = (r + 1 - 2 * core, c)
    greet(other)
    for k in (1, 2, 3, 4):
        greet(zdev(k))
        greet(zdev(-k))
    for k in range(1, NR // 2):
        greet(row_dev(k))

    points = pts[...]
    half = points.shape[0] // 2
    rp[c] = points
    scaled = -2.0 * points
    cp[0, core, y, x] = scaled[:half]
    cp[1, core, y, x] = scaled[half:]
    vr0[c] = t[...]
    vc0[core, yx] = t[...]
    zero = jnp.zeros((RHS, 2 * half), F32)
    fs[SLOTS] = zero
    bs[SLOTS] = zero
    pl.semaphore_wait(barrier, 1 + 8 + NR // 2 - 1)

    piece = points.shape[0] // PIECES

    def ring_copy(d, s, ch):
        sign = 1 - 2 * d
        part = rp.at[zidx(-sign * s), pl.ds(ch * piece, piece)]
        return rdma(part, part, ring_s.at[d, s, ch], ring_r.at[d, s, ch], zdev(sign))

    def ring_arrival(d, s, ch):
        sign = 1 - 2 * d
        part = rp.at[zidx(-sign * (s + 1)), pl.ds(ch * piece, piece)]
        return rdma(part, part, ring_s.at[d, s, ch], ring_r.at[d, s, ch], zdev(sign))

    def ring_has(d, s, ch):
        return s < 7 or ch // (PIECES // 2) == d

    def ring_start():
        for ch in range(PIECES):
            for d in range(2):
                ring_copy(d, 0, ch).start()

    def ring_forward(s):
        for ch in range(PIECES):
            for d in range(2):
                ring_arrival(d, s - 1, ch).wait_recv()
                if ring_has(d, s, ch):
                    ring_copy(d, s, ch).start()

    def ring_end():
        for ch in range(PIECES):
            for d in range(2):
                if ring_has(d, 7, ch):
                    ring_arrival(d, 7, ch).wait_recv()

    def xdev(k):
        return ((y * SIDE + lax.rem(x + k, SIDE)) * 2 + core, c)

    def ydev(k):
        return ((lax.rem(y + k, SIDE) * SIDE + x) * 2 + core, c)

    def wide(h, k, p, ref):
        return ref.at[0, k, p] if h == 0 else ref.at[1, k, :, p]

    def xy_first(h, k):
        mine = cp.at[h, core, y, x]
        return rdma(mine, mine, xy_s.at[h, 0, k], xy_r.at[h, 0, k], xdev(k) if h == 0 else ydev(k))

    def xy_second(h, k):
        group = wide(h, core, y if h == 0 else x, cp)
        return rdma(group, group, xy_s.at[h, 1, k], xy_r.at[h, 1, k], ydev(k) if h == 0 else xdev(k))

    def xy_third(h, k):
        place = lax.rem((y if h == 0 else x) + (SIDE - k), SIDE)
        group = wide(h, core, place, cp)
        return rdma(group, group, xy_s.at[h, 2, k], xy_r.at[h, 2, k], other)

    lane = lax.broadcasted_iota(jnp.int32, (half, 128), 1)

    def features(block, first, weight):
        wide32 = block.astype(F32)
        norm = jnp.sum(wide32 * wide32, axis=1, keepdims=True) * weight
        if not first:
            norm = norm + 1.0
        hi = norm.astype(BF16).astype(F32)
        mid = (norm - hi).astype(BF16).astype(F32)
        low = norm - hi - mid
        at = 0 if first else 3
        out = jnp.where(lane == at, hi, jnp.where(lane == at + 1, mid, jnp.where(lane == at + 2, low, 0.0)))
        one = 3 if first else 0
        out = jnp.where((lane >= one) & (lane < one + 3), 1.0, out)
        return out.astype(BF16)

    def row_features(block):
        for ch in range(2):
            part = pl.ds(ch * half, half)
            ra[block, part] = features(rp[block, part], True, 1.0)

    def col_features(h, k, p):
        for m in range(SIDE):
            if h == 0:
                ca[0, k, p, m] = features(cp[0, k, p, m], False, 0.25)
            else:
                ca[1, k, m, p] = features(cp[1, k, m, p], False, 0.25)

    ring_start()
    for k in (1, 3, 2):
        for h in range(2):
            xy_first(h, k).start()
    row_features(c)
    ring_forward(1)
    for h in range(2):
        for k in (1, 3, 2):
            xy_first(h, k).wait_recv()
        for k in (1, 3, 2):
            xy_second(h, k).start()
        xy_third(h, 0).start()
    ring_forward(2)
    for h in range(2):
        col_features(h, core, y if h == 0 else x)
    ring_forward(3)
    for d in range(2):
        for s in (1, 2):
            row_features(zidx(-(1 - 2 * d) * s))
    for h in range(2):
        xy_third(h, 0).wait_recv()
        col_features(h, 1 - core, y if h == 0 else x)
    ring_forward(4)
    for h in range(2):
        for k in (1, 3):
            xy_second(h, k).wait_recv()
            xy_third(h, k).start()
            col_features(h, core, lax.rem((y if h == 0 else x) + (SIDE - k), SIDE))
    ring_forward(5)
    for d in range(2):
        for s in (3, 4):
            row_features(zidx(-(1 - 2 * d) * s))
    for h in range(2):
        xy_second(h, 2).wait_recv()
        xy_third(h, 2).start()
    ring_forward(6)
    for h in range(2):
        col_features(h, core, lax.rem((y if h == 0 else x) + 2, SIDE))
    for h in range(2):
        for k in (1, 3):
            xy_third(h, k).wait_recv()
            col_features(h, 1 - core, lax.rem((y if h == 0 else x) + (SIDE - k), SIDE))
    ring_forward(7)

    def gather_z(n, buf):
        for d in range(2):
            for k in (4, 3, 2, 1):
                rdma(buf.at[c], buf.at[c], gz_s.at[n, d, k - 1], gz_r.at[n, d, k - 1], zdev((1 - 2 * d) * k)).start()

    def gather_z_far(n, d, k, buf):
        block = zidx(-(1 - 2 * d) * 4)
        part = buf.at[block] if k < 4 else buf.at[block, pl.ds(8 * d, 8)]
        return rdma(part, part, gz_s.at[n, d, 3 + k], gz_r.at[n, d, 3 + k], zdev((1 - 2 * d) * k))

    def gather_z_forward(n, buf):
        for d in range(2):
            rdma(buf.at[c], buf.at[c], gz_s.at[n, d, 3], gz_r.at[n, d, 3], zdev((1 - 2 * d) * 4)).wait_recv()
            for k in (4, 3, 2, 1):
                gather_z_far(n, d, k, buf).start()

    def gather_z_finish(n, buf):
        for d in range(2):
            for k in (1, 2, 3):
                rdma(buf.at[c], buf.at[c], gz_s.at[n, d, k - 1], gz_r.at[n, d, k - 1], zdev((1 - 2 * d) * k)).wait_recv()
            for k in (1, 2, 3, 4):
                gather_z_far(n, d, k, buf).wait_recv()

    def gather_z_sent(n, buf):
        for d in range(2):
            for k in (1, 2, 3, 4):
                rdma(buf.at[c], buf.at[c], gz_s.at[n, d, k - 1], gz_r.at[n, d, k - 1], zdev((1 - 2 * d) * k)).wait_send()
                gather_z_far(n, d, k, buf).wait_send()

    def gather_x(n, buf):
        for k in range(1, NR // 2):
            rdma(buf.at[core, yx], buf.at[core, yx], gx_s.at[n, 0], gx_r.at[n, 0], row_dev(k)).start()

    def gather_x_pair(n, buf):
        return rdma(buf.at[core], buf.at[core], gx_s.at[n, 1], gx_r.at[n, 1], other)

    def gather_x_forward(n, buf):
        drain(buf.at[core, pl.ds(0, NR // 2 - 1)], gx_r.at[n, 0])
        gather_x_pair(n, buf).start()

    def gather_x_sent(n, buf):
        drain(buf.at[core, pl.ds(0, NR // 2 - 1)], gx_s.at[n, 0])
        gather_x_pair(n, buf).wait_send()

    def place(d, k):
        return zidx((1 - 2 * d) * k)

    def scatter_z_far(n, d, k, part, za):
        block = place(d, k + 4)
        src = part.at[block] if k < 4 else part.at[block, pl.ds(8 * d, 8)]
        dst = za.at[d, k - 1] if k < 4 else za.at[d, 3, pl.ds(8 * d, 8)]
        return rdma(src, dst, sz_s.at[n, d, 3 + k], sz_r.at[n, d, 3 + k], zdev((1 - 2 * d) * k))

    def scatter_z_near(n, d, k, part, zb, zm):
        src = part.at[place(d, k)] if k < 4 else zm.at[d]
        return rdma(src, zb.at[d, k - 1], sz_s.at[n, d, k - 1], sz_r.at[n, d, k - 1], zdev((1 - 2 * d) * k))

    def scatter_z(n, part, za, zb, zm):
        for k in (4, 3, 2, 1):
            for d in range(2):
                scatter_z_far(n, d, k, part, za).start()
        for k in (3, 2, 1):
            for d in range(2):
                scatter_z_near(n, d, k, part, zb, zm).start()

    def scatter_z_forward(n, part, za, zb, zm):
        for d in range(2):
            for k in (1, 2, 3, 4):
                scatter_z_far(n, d, k, part, za).wait_recv()
            zm[d] = part[place(d, 4)] + za[d, 0] + za[d, 1] + za[d, 2]
            rowpart = pl.ds(8 * d, 8)
            zm[d, rowpart] = zm[d, rowpart] + za[d, 3, rowpart]
            scatter_z_near(n, d, 4, part, zb, zm).start()

    def scatter_z_finish(n, part, zb, zm):
        total = part[c]
        for k in (1, 2, 3, 4):
            for d in range(2):
                scatter_z_near(n, d, k, part, zb, zm).wait_recv()
                total = total + zb[d, k - 1]
        return total

    def scatter_z_sent(n, part, za, zb, zm):
        for d in range(2):
            for k in (1, 2, 3, 4):
                scatter_z_far(n, d, k, part, za).wait_send()
                scatter_z_near(n, d, k, part, zb, zm).wait_send()

    def scatter_x_pair(n, part, xs):
        return rdma(part.at[1 - core], xs, sx_s.at[n, 1], sx_r.at[n, 1], other)

    def scatter_x(n, part, xs, xi):
        scatter_x_pair(n, part, xs).wait_recv()
        for p in range(NR // 2):
            part[core, p] = part[core, p] + xs[p]
        for k in range(1, NR // 2):
            rdma(part.at[core, lax.rem(yx + k, NR // 2)], xi.at[yx], sx_s.at[n, 0], sx_r.at[n, 0], row_dev(k)).start()
        xi[yx] = part[core, yx]

    def scatter_x_finish(n, xi):
        drain(xi.at[pl.ds(0, NR // 2 - 1)], sx_r.at[n, 0])
        return total_of([xi[k] for k in range(NR // 2)])

    def scatter_x_sent(n, part, xs, xi):
        scatter_x_pair(n, part, xs).wait_send()
        drain(xi.at[pl.ds(0, NR // 2 - 1)], sx_s.at[n, 0])

    def reduce_z_copy(n, arz, block, rsem, k):
        return rdma(arz.at[block], arz.at[block], ar_s.at[n, 0], ar_r.at[n, rsem], zdev(k))

    def reduce_z(n, value, arz):
        arz[c] = value
        for k in (4, 3, 2, 1):
            for d in range(2):
                reduce_z_copy(n, arz, c, d if k == 4 else 2, (1 - 2 * d) * k).start()

    def reduce_z_forward(n, arz):
        for d in range(2):
            block = zidx(-(1 - 2 * d) * 4)
            reduce_z_copy(n, arz, block, d, 4).wait_recv()
            for k in (4, 3, 2, 1):
                if k < 4 or d == 0:
                    reduce_z_copy(n, arz, block, 2, (1 - 2 * d) * k).start()

    def reduce_pair(n, ars):
        return rdma(ars.at[core], ars.at[core], ar_s.at[n, 1], ar_r.at[n, 3], other)

    def reduce_cores(n, arz, ars):
        drain(arz.at[pl.ds(0, NC - 3)], ar_r.at[n, 2])
        ars[core] = jnp.sum(arz[...], axis=0)
        reduce_pair(n, ars).start()

    def reduce_x(n, ars, arx):
        reduce_pair(n, ars).wait_recv()
        arx[yx] = ars[0] + ars[1]
        for k in range(1, NR // 2):
            rdma(arx.at[yx], arx.at[yx], ar_s.at[n, 2], ar_r.at[n, 4], row_dev(k)).start()

    def reduce_finish(n, arx):
        drain(arx.at[pl.ds(0, NR // 2 - 1)], ar_r.at[n, 4])
        return jnp.sum(arx[...], axis=0)

    def reduce_sent(n, arz, ars, arx):
        drain(arz.at[pl.ds(0, NC - 1)], ar_s.at[n, 0])
        reduce_pair(n, ars).wait_send()
        drain(arx.at[pl.ds(0, NR // 2 - 1)], ar_s.at[n, 2])

    def make_tile(s, carry):
        a, q = meta[0, s], meta[1, s]
        k, pos = lax.rem(q, 2), q // 2
        qy, qx = pos // SIDE, lax.rem(pos, SIDE)
        right = jnp.concatenate([
            jnp.concatenate([cp[h, k, qy, qx], ca[h, k, qy, qx]], axis=1) for h in range(2)], axis=0)
        for h in range(2):
            part = pl.ds(h * half, half)
            left = jnp.concatenate([rp[a, part], ra[a, part]], axis=1)
            squared = jnp.maximum(lax.dot_general(left, right, NT, preferred_element_type=F32), 1.0)
            dist = squared * lax.rsqrt(squared)
            w = jnp.maximum(radius - dist, 0.0)
            w = w * w
            value = w * w * (dist + 0.25 * radius)
            hi = value.astype(BF16)
            khi[s, part] = hi
            klo[s, part] = (value - hi.astype(F32)).astype(BF16)
        return carry

    def split(v):
        hi = v.astype(BF16)
        return jnp.concatenate([hi, (v - hi.astype(F32)).astype(BF16)], axis=0)

    def apply(v, s, dims):
        both = lax.dot_general(v, khi[s], dims, preferred_element_type=F32)
        low = lax.dot_general(v[:RHS], klo[s], dims, preferred_element_type=F32)
        return both[:RHS] + both[RHS:] + low

    def forward(s, carry):
        q = meta[1, s]
        fs[s] = apply(wc[lax.rem(q, 2), q // 2], s, NT)
        return carry

    def backward(s, carry):
        bs[s] = apply(wr[meta[4, s]], meta[5, s], NN)
        return carry

    def add_up(buf, key):
        def one(j, carry):
            lanes = pl.ds(pl.multiple_of(j * 128, 128), 128)
            for g in range(RHS // 8):
                part = pl.ds(8 * g, 8)
                value = [buf[s, part, lanes] for s in range(SLOTS)]
                step = 1
                while step < SLOTS:
                    for s in range(SLOTS - 1, step - 1, -1):
                        same = meta[key, s] == meta[key, s - step]
                        value[s] = value[s] + jnp.where(same, value[s - step], 0.0)
                    step *= 2
                for s in range(SLOTS):
                    buf[s, part, lanes] = value[s]
            return carry
        lax.fori_loop(0, 2 * half // 128, one, 0)

    def sum_rows(part):
        add_up(fs, 2)
        for a in range(NC):
            part[a] = fs[meta[7, a]]

    def sum_cols(part):
        add_up(bs, 6)
        for q in range(NR):
            part[q % 2, q // 2] = bs[meta[8, q]]

    def curvature(vec):
        def add(s, total):
            weight = meta[3, s]
            product = vec[meta[0, s]] * fs[s]
            return total + jnp.where(weight > 0, jnp.where(weight > 1, 2.0, 1.0) * product, 0.0)
        return lax.fori_loop(0, SLOTS, add, jnp.zeros((RHS, 2 * half), F32), unroll=8)

    def along(value):
        return jnp.sum(value, axis=1, keepdims=True)

    column = lax.broadcasted_iota(jnp.int32, (RHS, 128), 1)

    sub = lax.broadcasted_iota(jnp.int32, (RHS, 128), 0)

    def as_row(value, n):
        return jnp.sum(jnp.where(column == sub + n * RHS, value, 0.0), axis=0, keepdims=True)

    def pick(row, n):
        return along(jnp.where(column == sub + n * RHS, row, 0.0))

    gather_z(0, vr0)
    gather_x(0, vc0)
    for d in range(2):
        for s in (5, 6):
            row_features(zidx(-(1 - 2 * d) * s))
    for h in range(2):
        xy_third(h, 2).wait_recv()
        col_features(h, 1 - core, lax.rem((y if h == 0 else x) + 2, SIDE))
    row_features(zidx(7))
    row_features(zidx(-7))
    ring_end()
    row_features(zidx(8))
    lax.fori_loop(0, SLOTS // 2, make_tile, 0)
    gather_z_forward(0, vr0)
    gather_x_forward(0, vc0)
    lax.fori_loop(SLOTS // 2, SLOTS, make_tile, 0)
    gather_z_finish(0, vr0)
    gather_x_pair(0, vc0).wait_recv()

    def split_all(vr, vc):
        def row(a, carry):
            wr[a] = split(vr[a])
            return carry

        def col(a, carry):
            for k in range(2):
                wc[k, a] = split(vc[k, a])
            return carry

        return (lambda: lax.fori_loop(0, NC, row, 0, unroll=4)), (lambda: lax.fori_loop(0, NR // 2, col, 0, unroll=2))

    split_rows, split_cols = split_all(vr0, vc0)
    split_cols()
    lax.fori_loop(0, SLOTS, forward, 0, unroll=8)
    target = t[...]
    curve = scale * along(curvature(vr0)) + along(noise[...] * target * target)
    reduce_z(0, as_row(curve, 0) + as_row(along(target * target), 1), arz0)
    sum_rows(rpart0)
    scatter_z(0, rpart0, za0, zb0, zm0)
    split_rows()
    lax.fori_loop(0, SLOTS, backward, 0, unroll=4)
    reduce_z_forward(0, arz0)
    sum_cols(cpart0)
    scatter_x_pair(0, cpart0, xs0).start()
    scatter_z_forward(0, rpart0, za0, zb0, zm0)
    reduce_cores(0, arz0, ars0)
    scatter_x(0, cpart0, xs0, xi0)
    reduce_x(0, ars0, arx0)
    image = scatter_z_finish(0, rpart0, zb0, zm0)
    image = noise[...] * target + scale * (image + scatter_x_finish(0, xi0))
    sums = reduce_finish(0, arx0)
    curve0 = pick(sums, 0)
    norm0 = pick(sums, 1)
    alpha0 = norm0 / curve0
    residual = target - alpha0 * image
    sol[...] = image
    vr1[c] = residual
    vc1[core, yx] = residual

    gather_x(1, vc1)
    gather_z(1, vr1)
    crossed = along(residual * image)
    squares = along(residual * residual)
    curve = along(noise[...] * residual * residual)
    split_rows, split_cols = split_all(vr1, vc1)
    gather_z_forward(1, vr1)
    gather_x_forward(1, vc1)
    gather_x_pair(1, vc1).wait_recv()
    split_cols()
    lax.fori_loop(0, SLOTS, forward, 0, unroll=8)
    gather_z_finish(1, vr1)
    curve = scale * along(curvature(vr1)) + curve
    reduce_z(1, as_row(curve, 0) + as_row(crossed, 1) + as_row(squares, 2), arz1)
    sum_rows(rpart1)
    scatter_z(1, rpart1, za1, zb1, zm1)
    split_rows()
    lax.fori_loop(0, SLOTS, backward, 0, unroll=4)
    reduce_z_forward(1, arz1)
    sum_cols(cpart1)
    scatter_x_pair(1, cpart1, xs1).start()
    scatter_z_forward(1, rpart1, za1, zb1, zm1)
    reduce_cores(1, arz1, ars1)
    scatter_x(1, cpart1, xs1, xi1)
    reduce_x(1, ars1, arx1)
    image = scatter_z_finish(1, rpart1, zb1, zm1)
    image = image + scatter_x_finish(1, xi1)
    sums = reduce_finish(1, arx1)
    norm1 = pick(sums, 2)
    beta = norm1 / norm0
    curve1 = pick(sums, 0) + beta * (2.0 * pick(sums, 1) + beta * curve0)
    alpha1 = norm1 / curve1
    residual = vr1[c]
    image = noise[...] * residual + scale * image + beta * sol[...]
    sol[...] = alpha0 * target + alpha1 * (residual + beta * target)
    res[...] = residual - alpha1 * image

    for s in range(8):
        for ch in range(PIECES):
            for d in range(2):
                if ring_has(d, s, ch):
                    ring_copy(d, s, ch).wait_send()
    for h in range(2):
        for k in (1, 2, 3):
            xy_first(h, k).wait_send()
            xy_second(h, k).wait_send()
        for k in range(4):
            xy_third(h, k).wait_send()
    gather_z_sent(0, vr0)
    gather_z_sent(1, vr1)
    gather_x_sent(0, vc0)
    gather_x_sent(1, vc1)
    scatter_z_sent(0, rpart0, za0, zb0, zm0)
    scatter_z_sent(1, rpart1, za1, zb1, zm1)
    scatter_x_sent(0, cpart0, xs0, xi0)
    scatter_x_sent(1, cpart1, xs1, xi1)
    reduce_sent(0, arz0, ars0, arx0)
    reduce_sent(1, arz1, ars1, arx1)


def plan(rows, cols, count):
    slot = jnp.arange(SLOTS, dtype=jnp.int32)
    a, q = rows % NC, cols // NC
    valid = slot < count
    mirrored = valid & (rows != cols)
    key_row = jnp.where(valid, a, NC)
    key_col = jnp.where(mirrored, q, NR)

    def order(key):
        full = key * SLOTS + slot
        rank = jnp.sum((full[None, :] < full[:, None]).astype(jnp.int32), axis=1)
        return rank, (rank[:, None] == slot[None, :]).astype(jnp.int32)

    def last(key):
        at_most = jnp.sum((key[:, None] <= slot[None, :]).astype(jnp.int32), axis=0)
        return jnp.where(jnp.any(key[:, None] == slot[None, :], axis=0), at_most - 1, SLOTS)

    rank_row, hot_row = order(key_row)
    _, hot_col = order(key_col)
    weight = valid.astype(jnp.int32) + mirrored.astype(jnp.int32)
    first = jnp.sum(jnp.stack([a, q, key_row, weight])[:, :, None] * hot_row[None], axis=1)
    second = jnp.sum(jnp.stack([a, rank_row, key_col])[:, :, None] * hot_col[None], axis=1)
    return jnp.concatenate([first, second, last(key_row)[None], last(key_col)[None]], axis=0)


def local(points, noise, targets, tile_rows, tile_cols, tile_count):
    block, width = points.shape
    radius = 2.8 * math.sqrt(width)
    scale = 2.0 / block * 4.0 / radius**5
    half = block // 2
    vmem = pl.BlockSpec(memory_space=pltpu.VMEM)
    smem = pl.BlockSpec(memory_space=pltpu.SMEM)
    vec = jax.ShapeDtypeStruct((RHS, block), F32)
    dma = pltpu.SemaphoreType.DMA

    def vecs(*lead):
        return pltpu.VMEM((*lead, RHS, block), F32)

    sol, res = pl.pallas_call(
        functools.partial(kernel, radius, scale),
        out_shape=(vec, vec),
        in_specs=[vmem, vmem, vmem, smem],
        out_specs=(vmem, vmem),
        scratch_shapes=[
            pltpu.VMEM((NC, block, width), BF16),
            pltpu.VMEM((NC, block, width), BF16),
            pltpu.VMEM((2, 2, SIDE, SIDE, half, width), BF16),
            pltpu.VMEM((2, 2, SIDE, SIDE, half, width), BF16),
            pltpu.VMEM((SLOTS, block, block), BF16),
            pltpu.VMEM((SLOTS, block, block), BF16),
            vecs(NC), vecs(2, NR // 2), vecs(NC), vecs(2, NR // 2),
            pltpu.VMEM((NC, 2 * RHS, block), BF16),
            pltpu.VMEM((2, NR // 2, 2 * RHS, block), BF16),
            vecs(SLOTS + 1), vecs(SLOTS + 1),
            vecs(NC), vecs(2, NR // 2), vecs(NC), vecs(2, NR // 2),
            vecs(2, 4), vecs(2, 4), vecs(2), vecs(NR // 2), vecs(NR // 2),
            vecs(2, 4), vecs(2, 4), vecs(2), vecs(NR // 2), vecs(NR // 2),
            *[pltpu.VMEM((n, 1, 128), F32) for n in (NC, 2, NR // 2) * 2],
            dma((2, 8, PIECES)), dma((2, 8, PIECES)),
            dma((2, 3, 4)), dma((2, 3, 4)),
            dma((2, 2, 8)), dma((2, 2, 8)),
            dma((2, 2)), dma((2, 2)),
            dma((2, 2, 8)), dma((2, 2, 8)),
            dma((2, 2)), dma((2, 2)),
            dma((2, 3)), dma((2, 5)),
        ],
        compiler_params=pltpu.CompilerParams(
            collective_id=0, has_side_effects=True, vmem_limit_bytes=60 * 1024 * 1024),
    )(points, noise[None, :], targets.T, plan(tile_rows[0, 0], tile_cols[0, 0], tile_count[0, 0]))
    return sol.T, res.T


def solution(mesh):
    return jax.shard_map(
        local,
        mesh=mesh,
        in_specs=(
            P(("row", "col"), None),
            P(("row", "col")),
            P(("row", "col"), None),
            P("row", "col", None),
            P("row", "col", None),
            P("row", "col"),
        ),
        out_specs=(P(("row", "col"), None), P(("row", "col"), None)),
        check_vma=False,
    )
```

time: 208 us -> 155 us (0.75)
  Pallas kernels: 204 us -> 149 us
    pallas_call x1, Pallas kernels: 204 us -> 149 us  [local(): pl.pallas_call(functools.partial(kernel, radius, scale), out_shape=(vec,...]
where the time goes in v2:
time: 155 us
  Pallas kernels  149 us (96%)
  local copies, waits for them, and re-layouts  2.65 us (2%)
    pallas_call x1, Pallas kernels, local(): pl.pallas_call(functools.partial(kernel, radius, scale), out_shape=(vec,...  149 us

profile of v2, /device:TPU:1, one launch (start us, length us, event | category | flops | bytes accessed | tf_op | source)
XLA Modules:
  0.0 154.5 jit_solution(15632616963264926035)
XLA Ops:
  1.3 0.0 copy-start.1
  1.3 0.0 copy-start.2
  1.3 0.6 copy-done.1
  1.9 0.0 copy-done.2
  2.0 0.2 convert_reduce_fusion.2
  2.1 0.1 fusion.2
  2.2 0.1 convert_reduce_fusion
  2.4 0.1 fusion.1
  2.5 0.1 multiply_reduce_fusion.1
  2.6 0.1 fusion
  2.7 0.1 multiply_reduce_fusion
  2.8 0.6 pad_add_fusion.meta
  3.4 149.1 %shard_map.77 = (f32[16,512]{1,0:T(8,128)}, f32[16,512]{1,0:T(8,128)}) custom-call(bf16[512,128]{1,0:T(8,128)(2,1)} %pts.1, f32[1,512]{1,0:T(1,128)} %bitcast.52, f32[16,512]{1,0:T(8,128)} %bitcast.50, s32[9,32]{1,0:T(8,128)} %pad_add_fusion.meta), custom_call_target="tpu_custom_call" | custom-call | tf_op jit(solution)/shard_map/pallas_call | solution.py:596
  152.5 0.0 copy-start
  152.5 1.4 copy.11
  153.9 0.0 copy-done
  153.9 0.6 copy.12
  (6 shorter events, 0.1 us)
Async XLA Ops:
  1.3 0.7 copy-start.1
  1.3 0.7 copy-start.2
  152.5 1.4 copy-start

commit v3 on v2

--- a/solution.py
+++ b/solution.py
@@ -448,10 +448,10 @@
     row_features(zidx(-7))
     ring_end()
     row_features(zidx(8))
-    lax.fori_loop(0, SLOTS // 2, make_tile, 0)
+    lax.fori_loop(0, SLOTS // 2, make_tile, 0, unroll=4)
     gather_z_forward(0, vr0)
     gather_x_forward(0, vc0)
-    lax.fori_loop(SLOTS // 2, SLOTS, make_tile, 0)
+    lax.fori_loop(SLOTS // 2, SLOTS, make_tile, 0, unroll=4)
     gather_z_finish(0, vr0)
     gather_x_pair(0, vc0).wait_recv()
 
@@ -476,7 +476,7 @@
     sum_rows(rpart0)
     scatter_z(0, rpart0, za0, zb0, zm0)
     split_rows()
-    lax.fori_loop(0, SLOTS, backward, 0, unroll=4)
+    lax.fori_loop(0, SLOTS, backward, 0, unroll=8)
     reduce_z_forward(0, arz0)
     sum_cols(cpart0)
     scatter_x_pair(0, cpart0, xs0).start()
@@ -512,7 +512,7 @@
     sum_rows(rpart1)
     scatter_z(1, rpart1, za1, zb1, zm1)
     split_rows()
-    lax.fori_loop(0, SLOTS, backward, 0, unroll=4)
+    lax.fori_loop(0, SLOTS, backward, 0, unroll=8)
     reduce_z_forward(1, arz1)
     sum_cols(cpart1)
     scatter_x_pair(1, cpart1, xs1).start()

time: 155 us -> 148 us (0.955)
  Pallas kernels: 149 us -> 143 us
    pallas_call x1, Pallas kernels: 149 us -> 143 us  [local(): pl.pallas_call(functools.partial(kernel, radius, scale), out_shape=(vec,...]
where the time goes in v3:
time: 148 us
  Pallas kernels  143 us (97%)
  local copies, waits for them, and re-layouts  2.65 us (2%)
    pallas_call x1, Pallas kernels, local(): pl.pallas_call(functools.partial(kernel, radius, scale), out_shape=(vec,...  143 us

profile of v3, /device:TPU:1, one launch (start us, length us, event | category | flops | bytes accessed | tf_op | source)
XLA Modules:
  0.0 148.3 jit_solution(5135795616638826562)
XLA Ops:
  1.3 0.0 copy-start.1
  1.3 0.0 copy-start.2
  1.3 0.6 copy-done.1
  1.9 0.0 copy-done.2
  2.0 0.2 convert_reduce_fusion.2
  2.1 0.1 fusion.2
  2.2 0.1 convert_reduce_fusion
  2.4 0.1 fusion.1
  2.5 0.1 multiply_reduce_fusion.1
  2.6 0.1 fusion
  2.7 0.1 multiply_reduce_fusion
  2.8 0.6 pad_add_fusion.meta
  3.4 142.9 %shard_map.77 = (f32[16,512]{1,0:T(8,128)}, f32[16,512]{1,0:T(8,128)}) custom-call(bf16[512,128]{1,0:T(8,128)(2,1)} %pts.1, f32[1,512]{1,0:T(1,128)} %bitcast.52, f32[16,512]{1,0:T(8,128)} %bitcast.50, s32[9,32]{1,0:T(8,128)} %pad_add_fusion.meta), custom_call_target="tpu_custom_call" | custom-call | tf_op jit(solution)/shard_map/pallas_call | solution.py:596
  146.2 0.0 copy-start
  146.3 1.4 copy.11
  147.6 0.0 copy-done
  147.6 0.6 copy.12
  (6 shorter events, 0.1 us)
Async XLA Ops:
  1.3 0.7 copy-start.1
  1.3 0.7 copy-start.2
  146.2 1.4 copy-start
